TPU v7x, 256 devices: a whole 4x4x8 slice. The times are simulated.
256 devices in a mesh: dp: 64 (over z, x, core), group: 4 (over y).
Axes of the slice: x: 4, y: 4, z: 8, core: 2. Of those that a mesh axis runs over, the one named last changes fastest.
Arguments:
- frames: bfloat16 [64, 4, 384, 8192], P('dp', 'group'), may hold values from -6 to 6
- lengths: int32 [64, 4, 4], P('dp', 'group'), may hold values from 32 to 96, as said below
- probes: bfloat16 [8192, 256], P('dp'), may hold values from -0.0625 to 0.0625
Outputs:
- basis: float32 [8192, 256], P('dp')
- factor: float32 [256, 256], replicated
Inputs may be any that keep to these rules, and one draw needn't show every extreme that they name: `lengths`: each device's spans lie back to back from its first frame slot; the device at index 0 of both axes has all 4 spans of length 96.
All inputs are finite; a program needn't handle non-finite values.
Results may differ from a plain program's by a relative error of at most 0.0031.
Values may be sent and summed in bfloat16 or wider, within the bound.
A program may use at most 128 MiB of HBM per device.

v0:
```python
import math
import jax
import jax.numpy as jnp
from jax import lax
from jax.sharding import PartitionSpec as P


def pair_mask(lengths, count):
    ends = jnp.cumsum(lengths)
    starts = ends - lengths
    position = jnp.arange(count, dtype=jnp.int32)
    inside = (position[:, None] >= starts[None, :] + 1) & (position[:, None] <= ends[None, :] - 1)
    return jnp.any(inside, axis=1)


def shards(frames, lengths, probes):
    local = frames.reshape(frames.shape[2], frames.shape[3])
    sizes = lengths.reshape(lengths.shape[2])
    count = local.shape[0]
    width = local.shape[1]
    columns = probes.shape[1]
    devices = lax.axis_size("dp") * lax.axis_size("group")
    scale = 1.0 / math.sqrt(width * count * devices)
    cols = local
    projected = jnp.dot(
        cols, lax.all_gather(probes, "dp", axis=0, tiled=True), preferred_element_type=jnp.float32
    ).astype(jnp.bfloat16)
    shifted = jnp.concatenate([jnp.zeros((1, columns), jnp.bfloat16), projected[:-1]], axis=0)
    paired = jnp.where(pair_mask(sizes, count)[:, None], shifted, jnp.zeros_like(shifted))
    contract = (((0,), (0,)), ((), ()))
    cols = local
    owned = lax.psum_scatter(
        scale * lax.dot_general(cols, paired, contract, preferred_element_type=jnp.float32),
        "dp",
        scatter_dimension=0,
        tiled=True,
    )
    sketch = lax.psum(owned, "group")
    local_gram = jnp.dot(sketch.T, sketch, precision=lax.Precision.HIGHEST)
    gram = lax.psum(local_gram, "dp")
    lower = jnp.linalg.cholesky(gram)
    basis = jax.scipy.linalg.solve_triangular(lower, sketch.T, lower=True).T * math.sqrt(width)
    return (basis, lower.T)


def solution(mesh):
    placed = (P("dp", "group", None, None), P("dp", "group", None), P("dp", None))
    return jax.shard_map(
        shards, mesh=mesh, in_specs=placed, out_specs=(P("dp", None), P()), check_vma=False
    )
```

profile of v0, /device:TPU:1, one launch (start us, length us, event | category | flops | bytes accessed | tf_op | source)
XLA Modules:
  0.0 553.6 jit_solution(10978117318791723454)
XLA Ops:
  7.2 0.7 all-gather.2.cloned.1.call-update
  7.9 0.8 reduce-window.7
  8.8 0.7 fusion.21
  9.4 0.1 fusion.20
  9.5 84.5 %all-gather.2.cloned.1.call-done = bf16[8192,256]{1,0:T(8,128)(2,1)} async-done(((bf16[128,256]{1,0:T(8,128)(2,1)}), bf16[8192,256]{1,0:T(8,128)(2,1)}) %all-gather.2.cloned.1.call-update) | async-done | bytes 4194320 | tf_op jit(solution)/shard_map/all_gather | solution.py:26
  94.0 5.9 %fusion.2 = bf16[384,256]{1,0:T(8,128)(2,1)S(1)} fusion(bf16[8192,256]{1,0:T(8,128)(2,1)} %all-gather.2.cloned.1.call-done, bf16[1,1,384,8192]{3,2,1,0:T(8,128)(2,1)} %param.3), kind=kOutput, calls=%fused_computation.5 | convolution fusion | flops 1610612736 | bytes 10682368 | tf_op jit(solution)/shard_map/dot_general | solution.py:25
  99.9 5.7 %fusion = f32[8192,256]{0,1:T(8,128)} fusion(bf16[1,1,384,8192]{3,2,1,0:T(8,128)(2,1)S(1)} %copy-done, bf16[383,256]{1,0:T(8,128)(2,1)S(1)} %bitcast.57, pred[384]{0:T(512)(128)(4,1)S(1)} %fusion.20), kind=kOutput, calls=%fused_computation.3 | convolution fusion | flops 1612808192 | bytes 14876544 | tf_op jit(solution)/shard_map/dot_general | solution.py:33
  105.7 143.7 %reduce-scatter.2.cloned.1.call-done = f32[128,256]{0,1:T(8,128)} async-done(((f32[8192,256]{0,1:T(8,128)}), f32[128,256]{0,1:T(8,128)}) %reduce-scatter.2.cloned.1.call-update) | async-done | bytes 131088 | tf_op jit(solution)/shard_map/reduce_scatter | solution.py:32
  249.4 0.2 all-reduce.7.cloned.1.call-start
  249.6 49.4 %all-reduce.5.cloned.1.call-done = f32[128,256]{0,1:T(8,128)} async-done(((f32[128,256]{0,1:T(8,128)}), f32[128,256]{0,1:T(8,128)}) %all-reduce.5.cloned.1.call-update) | async-done | bytes 131088 | tf_op jit(solution)/shard_map/psum | solution.py:38
  299.0 2.1 fusion.24
  301.2 179.8 %all-reduce.7.cloned.1.call-done = f32[256,256]{0,1:T(8,128)} async-done(((f32[256,256]{0,1:T(8,128)}), f32[256,256]{0,1:T(8,128)}) %all-reduce.7.cloned.1.call-update) | async-done | bytes 262160 | tf_op jit(solution)/shard_map/psum | solution.py:40
  480.9 1.1 copy.10
  482.0 1.0 fusion.4
  483.0 11.7 %cholesky.50 = f32[128,128]{1,0:T(8,128)S(1)} custom-call(f32[128,128]{1,0:T(8,128)S(1)} %cholesky.118), custom_call_target="Cholesky" | custom-call | tf_op jit(solution)/shard_map/jit(cholesky)/cholesky | solution.py:41
  494.8 9.8 %custom-call.15 = f32[1,128,128]{1,2,0:T(8,128)S(1)} custom-call(f32[1,128,128]{2,1,0:T(8,128)S(1)} %get-tuple-element.29), custom_call_target="InvertDiagBlocksLowerTriangular" | custom-call | tf_op jit(solution)/shard_map/jit(cholesky)/cholesky | solution.py:41
  504.6 0.2 constant_dynamic-update-slice_fusion.1
  504.8 0.3 convolution_subtract_fusion.1
  505.1 11.7 %cholesky.105 = f32[128,128]{1,0:T(8,128)S(1)} custom-call(f32[128,128]{1,0:T(8,128)S(1)} %convolution_subtract_fusion.1), custom_call_target="Cholesky" | custom-call | tf_op jit(solution)/shard_map/jit(cholesky)/cholesky | solution.py:41
  516.9 0.7 compare_reduce_fusion
  519.0 0.1 triangular_solve.57
  519.0 4.3 while.1
  519.2 0.6 fusion.33
  519.8 1.4 bitcast_dynamic-update-slice_fusion.2
  521.3 0.6 fusion.33
  521.9 1.4 bitcast_dynamic-update-slice_fusion.2
  523.3 19.7 %custom-call.16 = f32[2,128,128]{1,2,0:T(8,128)S(1)} custom-call(f32[2,128,128]{2,1,0:T(8,128)S(1)} %get-tuple-element.9), custom_call_target="InvertDiagBlocksLowerTriangular" | custom-call | tf_op jit(solution)/shard_map/jit(_solve_triangular)/triangular_solve | solution.py:42
  543.0 1.1 fusion.14
  544.1 1.0 convolution_subtract_fusion
  545.2 0.3 fusion.13
  545.5 0.8 copy.11
  546.3 0.8 copy.12
  (18 shorter events, 0.3 us)
Async XLA Ops:
  7.2 86.8 %all-gather.2.cloned.1.call-start = ((), (), s32[]{:S(2)}) async-start(), calls=%async_computation.1 | async-start | bytes 4259840 | tf_op jit(solution)/shard_map/all_gather | solution.py:26
  7.9 241.5 %reduce-scatter.2.cloned.1.call-start = ((), (), s32[]{:S(2)}) async-start(), calls=%async_computation.2 | async-start | bytes 8519680 | tf_op jit(solution)/shard_map/reduce_scatter | solution.py:32
  94.0 5.9 %copy-start = (bf16[1,1,384,8192]{3,2,1,0:T(8,128)(2,1)S(1)}, bf16[1,1,384,8192]{3,2,1,0:T(8,128)(2,1)}, u32[]{:S(2)}) copy-start(bf16[1,1,384,8192]{3,2,1,0:T(8,128)(2,1)} %param.3) | copy-start | bytes 18874372
  105.6 193.4 %all-reduce.5.cloned.1.call-start = ((), (), s32[]{:S(2)}) async-start(), calls=%async_computation.3 | async-start | bytes 262144 | tf_op jit(solution)/shard_map/psum | solution.py:38
  249.4 231.5 %all-reduce.7.cloned.1.call-start = ((), (), s32[]{:S(2)}) async-start(), calls=%async_computation.4 | async-start | bytes 524288 | tf_op jit(solution)/shard_map/psum | solution.py:40
Sparse Core Ops, SparseCore 0:
  10.8 83.1 all-gather.1
  105.8 143.5 reduce-scatter.1
  251.8 47.1 all-reduce.4
  302.9 177.9 all-reduce.6
where the time goes:
time: 554 us
  waiting for transfers between devices  458 us (83%)
  other arithmetic  56.3 us (10%)
  matrix products  16.6 us (3%)
  between operations  15.2 us (3%)
  local copies, waits for them, and re-layouts  6.83 us (1%)
    psum x1, waiting for transfers between devices, shards(): gram = lax.psum(local_gram, 'dp')  180 us
    reduce_scatter x1, waiting for transfers between devices, shards(): lax.psum_scatter(scale * lax.dot_general(cols, paired, contract, preferre...  144 us
    all_gather x1, waiting for transfers between devices, shards(): lax.all_gather(probes, 'dp', axis=0, tiled=True)  84.5 us
    psum x1, waiting for transfers between devices, shards(): sketch = lax.psum(owned, 'group')  49.4 us
    another operation x6, other arithmetic, shards(): lower = jnp.linalg.cholesky(gram)  34 us
    another operation x2, other arithmetic, shards(): jax.scipy.linalg.solve_triangular(lower, sketch.T, lower=True)  19.7 us
  transfers between devices with their start and end apart: 4, of which 4 were waited for; matrix products, arithmetic and copies ran while one was open for 0% of the time, Pallas kernels for 0%

commit v1 on v0

--- a/solution.py
+++ b/solution.py
@@ -23,7 +23,11 @@
     scale = 1.0 / math.sqrt(width * count * devices)
     cols = local
     projected = jnp.dot(
-        cols, lax.all_gather(probes, "dp", axis=0, tiled=True), preferred_element_type=jnp.float32
+        cols,
+        jnp.concatenate(
+            lax.all_to_all(jnp.stack([probes] * lax.axis_size("dp")), "dp", 0, 0), axis=0
+        ),
+        preferred_element_type=jnp.float32,
     ).astype(jnp.bfloat16)
     shifted = jnp.concatenate([jnp.zeros((1, columns), jnp.bfloat16), projected[:-1]], axis=0)
     paired = jnp.where(pair_mask(sizes, count)[:, None], shifted, jnp.zeros_like(shifted))

time: 554 us -> 579 us (1.045)
  starting transfers between devices: 0.34 us -> 13.6 us
  waiting for transfers between devices: 458 us -> 468 us
    all_to_all x0 -> x1, waiting for transfers between devices: none -> 94.1 us  [shards(): lax.all_to_all(jnp.stack([probes] * lax.axis_size('dp')), 'dp', 0, 0)]
    all_gather x1 -> x0, waiting for transfers between devices: 84.5 us -> none  [shards(): lax.all_gather(probes, 'dp', axis=0, tiled=True)]
    all_to_all x0 -> x1, starting transfers between devices: none -> 13.3 us  [shards(): lax.all_to_all(jnp.stack([probes] * lax.axis_size('dp')), 'dp', 0, 0)]
where the time goes in v1:
time: 579 us
  waiting for transfers between devices  468 us (81%)
  other arithmetic  55 us (9%)
  matrix products  16.6 us (3%)
  between operations  15.3 us (3%)
  starting transfers between devices  13.6 us (2%)
  local copies, waits for them, and re-layouts  10.2 us (2%)
    psum x1, waiting for transfers between devices, shards(): gram = lax.psum(local_gram, 'dp')  180 us
    reduce_scatter x1, waiting for transfers between devices, shards(): lax.psum_scatter(scale * lax.dot_general(cols, paired, contract, preferre...  144 us
    all_to_all x1, waiting for transfers between devices, shards(): lax.all_to_all(jnp.stack([probes] * lax.axis_size('dp')), 'dp', 0, 0)  94.1 us
    psum x1, waiting for transfers between devices, shards(): sketch = lax.psum(owned, 'group')  49.4 us
    another operation x6, other arithmetic, shards(): lower = jnp.linalg.cholesky(gram)  34 us
    another operation x2, other arithmetic, shards(): jax.scipy.linalg.solve_triangular(lower, sketch.T, lower=True)  19.7 us
    all_to_all x1, starting transfers between devices, shards(): lax.all_to_all(jnp.stack([probes] * lax.axis_size('dp')), 'dp', 0, 0)  13.3 us
  transfers between devices with their start and end apart: 4, of which 4 were waited for; matrix products, arithmetic and copies ran while one was open for 0% of the time, Pallas kernels for 0%

profile of v1, /device:TPU:1, one launch (start us, length us, event | category | flops | bytes accessed | tf_op | source)
XLA Modules:
  0.0 578.6 jit_solution(10561221820650746554)
XLA Ops:
  7.2 3.3 stack.2
  10.5 13.3 %all-to-all-start = ((bf16[64,128,256]{2,1,0:T(8,128)(2,1)}), bf16[64,128,256]{2,1,0:T(8,128)(2,1)}, u32[]{:S(2)}, u32[]{:S(2)}) async-start(bf16[64,128,256]{2,1,0:T(8,128)(2,1)} %stack.2), calls=%async_computation | async-start | bytes 8388608 | tf_op jit(solution)/shard_map/all_to_all | solution.py:28
  23.9 0.2 reduce-window.7
  24.1 0.1 fusion.20
  24.1 94.1 %all-to-all-done = bf16[64,128,256]{2,1,0:T(8,128)(2,1)} async-done(((bf16[64,128,256]{2,1,0:T(8,128)(2,1)}), bf16[64,128,256]{2,1,0:T(8,128)(2,1)}, u32[]{:S(2)}, u32[]{:S(2)}) %all-to-all-start) | async-done | bytes 4194336 | tf_op jit(solution)/shard_map/all_to_all | solution.py:28
  118.2 5.9 %fusion.2 = bf16[384,256]{1,0:T(8,128)(2,1)S(1)} fusion(bf16[8192,256]{1,0:T(8,128)(2,1)} %bitcast.4, bf16[1,1,384,8192]{3,2,1,0:T(8,128)(2,1)} %param.3), kind=kOutput, calls=%fused_computation.5 | convolution fusion | flops 1610612736 | bytes 10682368 | tf_op jit(solution)/shard_map/dot_general | solution.py:25
  124.2 5.7 fusion
  129.9 144.3 %reduce-scatter.2.cloned.1.call-done = f32[128,256]{0,1:T(8,128)} async-done(((f32[8192,256]{0,1:T(8,128)}), f32[128,256]{0,1:T(8,128)}) %reduce-scatter.2.cloned.1.call-update) | async-done | bytes 131088 | tf_op jit(solution)/shard_map/reduce_scatter | solution.py:36
  274.3 0.2 all-reduce.7.cloned.1.call-start
  274.5 49.4 %all-reduce.5.cloned.1.call-done = f32[128,256]{0,1:T(8,128)} async-done(((f32[128,256]{0,1:T(8,128)}), f32[128,256]{0,1:T(8,128)}) %all-reduce.5.cloned.1.call-update) | async-done | bytes 131088 | tf_op jit(solution)/shard_map/psum | solution.py:42
  323.9 2.1 fusion.24
  326.0 179.9 %all-reduce.7.cloned.1.call-done = f32[256,256]{0,1:T(8,128)} async-done(((f32[256,256]{0,1:T(8,128)}), f32[256,256]{0,1:T(8,128)}) %all-reduce.7.cloned.1.call-update) | async-done | bytes 262160 | tf_op jit(solution)/shard_map/psum | solution.py:44
  506.0 1.1 copy.10
  507.0 1.0 fusion.4
  508.0 11.7 %cholesky.50 = f32[128,128]{1,0:T(8,128)S(1)} custom-call(f32[128,128]{1,0:T(8,128)S(1)} %cholesky.118), custom_call_target="Cholesky" | custom-call | tf_op jit(solution)/shard_map/jit(cholesky)/cholesky | solution.py:45
  519.8 9.8 %custom-call.15 = f32[1,128,128]{1,2,0:T(8,128)S(1)} custom-call(f32[1,128,128]{2,1,0:T(8,128)S(1)} %get-tuple-element.29), custom_call_target="InvertDiagBlocksLowerTriangular" | custom-call | tf_op jit(solution)/shard_map/jit(cholesky)/cholesky | solution.py:45
  529.6 0.2 constant_dynamic-update-slice_fusion.1
  529.8 0.3 convolution_subtract_fusion.1
  530.1 11.7 %cholesky.105 = f32[128,128]{1,0:T(8,128)S(1)} custom-call(f32[128,128]{1,0:T(8,128)S(1)} %convolution_subtract_fusion.1), custom_call_target="Cholesky" | custom-call | tf_op jit(solution)/shard_map/jit(cholesky)/cholesky | solution.py:45
  541.9 0.7 compare_reduce_fusion
  544.0 0.1 triangular_solve.57
  544.1 4.3 while.1
  544.2 0.6 fusion.33
  544.8 1.4 bitcast_dynamic-update-slice_fusion.2
  546.3 0.6 fusion.33
  546.9 1.4 bitcast_dynamic-update-slice_fusion.2
  548.3 19.7 %custom-call.16 = f32[2,128,128]{1,2,0:T(8,128)S(1)} custom-call(f32[2,128,128]{2,1,0:T(8,128)S(1)} %get-tuple-element.9), custom_call_target="InvertDiagBlocksLowerTriangular" | custom-call | tf_op jit(solution)/shard_map/jit(_solve_triangular)/triangular_solve | solution.py:46
  568.0 1.1 fusion.14
  569.1 1.0 convolution_subtract_fusion
  570.2 0.3 fusion.13
  570.5 0.8 copy.11
  571.3 0.8 copy.12
  (23 shorter events, 0.3 us)
Async XLA Ops:
  7.2 16.7 %copy-start = (s32[1,1,4]{2,1,0:T(1,128)S(1)}, s32[1,1,4]{2,1,0:T(1,128)}, u32[]{:S(2)}) copy-start(s32[1,1,4]{2,1,0:T(1,128)} %param.4) | copy-start | bytes 52
  10.5 113.7 %slice-start = ((s8[6291456]{0:T(1024)(128)(4,1)}), s8[2097152]{0:T(1024)(128)(4,1)S(1)}, s32[]{:S(2)}) async-start(s8[6291456]{0:T(1024)(128)(4,1)} %bitcast.56), calls=%async_computation.5 | async-start | bytes 4194304
  10.5 107.7 %all-to-all-start = ((bf16[64,128,256]{2,1,0:T(8,128)(2,1)}), bf16[64,128,256]{2,1,0:T(8,128)(2,1)}, u32[]{:S(2)}, u32[]{:S(2)}) async-start(bf16[64,128,256]{2,1,0:T(8,128)(2,1)} %stack.2), calls=%async_computation | async-start | bytes 8388608 | tf_op jit(solution)/shard_map/all_to_all | solution.py:28
  23.8 250.5 %reduce-scatter.2.cloned.1.call-start = ((), (), s32[]{:S(2)}) async-start(), calls=%async_computation.2 | async-start | bytes 8519680 | tf_op jit(solution)/shard_map/reduce_scatter | solution.py:36
  118.2 6.0 %slice-start.1 = ((s8[6291456]{0:T(1024)(128)(4,1)}), s8[4194304]{0:T(1024)(128)(4,1)S(1)}, s32[]{:S(2)}) async-start(s8[6291456]{0:T(1024)(128)(4,1)} %bitcast.56), calls=%async_computation.6 | async-start | bytes 8388608
  129.9 194.0 %all-reduce.5.cloned.1.call-start = ((), (), s32[]{:S(2)}) async-start(), calls=%async_computation.3 | async-start | bytes 262144 | tf_op jit(solution)/shard_map/psum | solution.py:42
  274.3 231.7 %all-reduce.7.cloned.1.call-start = ((), (), s32[]{:S(2)}) async-start(), calls=%async_computation.4 | async-start | bytes 524288 | tf_op jit(solution)/shard_map/psum | solution.py:44
Sparse Core Ops, SparseCore 0:
  130.0 144.2 reduce-scatter.1
  276.7 47.1 all-reduce.4
  328.0 177.9 all-reduce.6

commit v2 on v0

--- a/solution.py
+++ b/solution.py
@@ -37,7 +37,7 @@
     )
     sketch = lax.psum(owned, "group")
     local_gram = jnp.dot(sketch.T, sketch, precision=lax.Precision.HIGHEST)
-    gram = lax.psum(local_gram, "dp")
+    gram = jnp.sum(lax.all_gather(local_gram, "dp"), axis=0)
     lower = jnp.linalg.cholesky(gram)
     basis = jax.scipy.linalg.solve_triangular(lower, sketch.T, lower=True).T * math.sqrt(width)
     return (basis, lower.T)

time: 554 us -> 481 us (0.87)
  waiting for transfers between devices: 458 us -> 382 us
  other arithmetic: 56.3 us -> 62.3 us
    psum x1 -> x0, waiting for transfers between devices: 180 us -> none  [shards(): gram = lax.psum(local_gram, 'dp')]
    all_gather x0 -> x1, waiting for transfers between devices: none -> 104 us  [shards(): gram = jnp.sum(lax.all_gather(local_gram, 'dp'), axis=0)]
    reduce_sum x0 -> x1, other arithmetic: none -> 6.89 us  [shards(): gram = jnp.sum(lax.all_gather(local_gram, 'dp'), axis=0)]
where the time goes in v2:
time: 481 us
  waiting for transfers between devices  382 us (79%)
  other arithmetic  62.3 us (13%)
  between operations  15.3 us (3%)
  matrix products  14.9 us (3%)
  local copies, waits for them, and re-layouts  5.88 us (1%)
    reduce_scatter x1, waiting for transfers between devices, shards(): lax.psum_scatter(scale * lax.dot_general(cols, paired, contract, preferre...  144 us
    all_gather x1, waiting for transfers between devices, shards(): gram = jnp.sum(lax.all_gather(local_gram, 'dp'), axis=0)  104 us
    all_gather x1, waiting for transfers between devices, shards(): lax.all_gather(probes, 'dp', axis=0, tiled=True)  84.5 us
    psum x1, waiting for transfers between devices, shards(): sketch = lax.psum(owned, 'group')  49.4 us
    another operation x6, other arithmetic, shards(): lower = jnp.linalg.cholesky(gram)  34 us
    another operation x2, other arithmetic, shards(): jax.scipy.linalg.solve_triangular(lower, sketch.T, lower=True)  19.7 us
  transfers between devices with their start and end apart: 4, of which 4 were waited for; matrix products, arithmetic and copies ran while one was open for 0% of the time, Pallas kernels for 0%

profile of v2, /device:TPU:1, one launch (start us, length us, event | category | flops | bytes accessed | tf_op | source)
XLA Modules:
  0.0 480.9 jit_solution(7462557500390459168)
XLA Ops:
  7.2 0.7 all-gather.4.cloned.1.call-update
  7.9 0.8 reduce-window.7
  8.8 0.7 fusion.21
  9.4 0.1 fusion.20
  9.5 84.5 %all-gather.4.cloned.1.call-done = bf16[8192,256]{1,0:T(8,128)(2,1)} async-done(((bf16[128,256]{1,0:T(8,128)(2,1)}), bf16[8192,256]{1,0:T(8,128)(2,1)}) %all-gather.4.cloned.1.call-update) | async-done | bytes 4194320 | tf_op jit(solution)/shard_map/all_gather | solution.py:26
  94.0 5.9 %fusion.2 = bf16[384,256]{1,0:T(8,128)(2,1)S(1)} fusion(bf16[8192,256]{1,0:T(8,128)(2,1)} %all-gather.4.cloned.1.call-done, bf16[1,1,384,8192]{3,2,1,0:T(8,128)(2,1)} %param.3), kind=kOutput, calls=%fused_computation.5 | convolution fusion | flops 1610612736 | bytes 10682368 | tf_op jit(solution)/shard_map/dot_general | solution.py:25
  99.9 5.7 %fusion = f32[8192,256]{0,1:T(8,128)} fusion(bf16[1,1,384,8192]{3,2,1,0:T(8,128)(2,1)S(1)} %copy-done, bf16[383,256]{1,0:T(8,128)(2,1)S(1)} %bitcast.59, pred[384]{0:T(512)(128)(4,1)S(1)} %fusion.20), kind=kOutput, calls=%fused_computation.3 | convolution fusion | flops 1612808192 | bytes 14876544 | tf_op jit(solution)/shard_map/dot_general | solution.py:33
  105.7 143.7 %reduce-scatter.2.cloned.1.call-done = f32[128,256]{0,1:T(8,128)} async-done(((f32[8192,256]{0,1:T(8,128)}), f32[128,256]{0,1:T(8,128)}) %reduce-scatter.2.cloned.1.call-update) | async-done | bytes 131088 | tf_op jit(solution)/shard_map/reduce_scatter | solution.py:32
  249.4 0.2 all-gather.6.cloned.1.call-start
  249.6 49.4 %all-reduce.4.cloned.1.call-done = f32[128,256]{0,1:T(8,128)} async-done(((f32[128,256]{0,1:T(8,128)}), f32[128,256]{0,1:T(8,128)}) %all-reduce.4.cloned.1.call-update) | async-done | bytes 131088 | tf_op jit(solution)/shard_map/psum | solution.py:38
  299.0 2.1 fusion.24
  301.2 103.7 %all-gather.6.cloned.1.call-done = f32[16384,256]{1,0:T(8,128)} async-done(((f32[256,256]{1,0:T(8,128)}), f32[16384,256]{1,0:T(8,128)}) %all-gather.6.cloned.1.call-update) | async-done | bytes 16777232 | tf_op jit(solution)/shard_map/all_gather | solution.py:40
  404.9 6.9 %reduce_sum.9 = f32[256,256]{1,0:T(8,128)S(1)} reduce(f32[64,256,256]{2,1,0:T(8,128)} %bitcast.56, f32[]{:T(128)} %constant.91.clone.1), dimensions={0}, to_apply=%region_4.5 | reduce | flops 4128768 | bytes 17039364 | tf_op jit(solution)/shard_map/reduce_sum | solution.py:40
  411.8 0.1 copy.11
  412.0 11.7 %cholesky.50 = f32[128,128]{1,0:T(8,128)S(1)} custom-call(f32[128,128]{1,0:T(8,128)S(1)} %cholesky.118), custom_call_target="Cholesky" | custom-call | tf_op jit(solution)/shard_map/jit(cholesky)/cholesky | solution.py:41
  423.8 9.8 %custom-call.15 = f32[1,128,128]{1,2,0:T(8,128)S(1)} custom-call(f32[1,128,128]{2,1,0:T(8,128)S(1)} %get-tuple-element.31), custom_call_target="InvertDiagBlocksLowerTriangular" | custom-call | tf_op jit(solution)/shard_map/jit(cholesky)/cholesky | solution.py:41
  433.6 0.2 constant_dynamic-update-slice_fusion.1
  433.8 0.3 convolution_subtract_fusion.1
  434.1 11.7 %cholesky.105 = f32[128,128]{1,0:T(8,128)S(1)} custom-call(f32[128,128]{1,0:T(8,128)S(1)} %convolution_subtract_fusion.1), custom_call_target="Cholesky" | custom-call | tf_op jit(solution)/shard_map/jit(cholesky)/cholesky | solution.py:41
  445.8 0.7 compare_reduce_fusion
  447.9 0.1 triangular_solve.57
  448.0 4.3 while.1
  448.2 0.6 fusion.33
  448.8 1.4 bitcast_dynamic-update-slice_fusion.2
  450.2 0.6 fusion.33
  450.8 1.4 bitcast_dynamic-update-slice_fusion.2
  452.3 19.7 %custom-call.16 = f32[2,128,128]{1,2,0:T(8,128)S(1)} custom-call(f32[2,128,128]{2,1,0:T(8,128)S(1)} %get-tuple-element.9), custom_call_target="InvertDiagBlocksLowerTriangular" | custom-call | tf_op jit(solution)/shard_map/jit(_solve_triangular)/triangular_solve | solution.py:42
  472.0 0.3 fusion.14
  472.2 0.2 convolution_subtract_fusion
  472.5 0.3 fusion.13
  472.8 0.8 copy.12
  473.5 0.8 copy.13
  (21 shorter events, 0.4 us)
Async XLA Ops:
  7.2 86.8 %all-gather.4.cloned.1.call-start = ((), (), s32[]{:S(2)}) async-start(), calls=%async_computation.1 | async-start | bytes 4259840 | tf_op jit(solution)/shard_map/all_gather | solution.py:26
  7.9 241.5 %reduce-scatter.2.cloned.1.call-start = ((), (), s32[]{:S(2)}) async-start(), calls=%async_computation.2 | async-start | bytes 8519680 | tf_op jit(solution)/shard_map/reduce_scatter | solution.py:32
  94.0 5.9 %copy-start = (bf16[1,1,384,8192]{3,2,1,0:T(8,128)(2,1)S(1)}, bf16[1,1,384,8192]{3,2,1,0:T(8,128)(2,1)}, u32[]{:S(2)}) copy-start(bf16[1,1,384,8192]{3,2,1,0:T(8,128)(2,1)} %param.3) | copy-start | bytes 18874372
  105.6 193.4 %all-reduce.4.cloned.1.call-start = ((), (), s32[]{:S(2)}) async-start(), calls=%async_computation.3 | async-start | bytes 262144 | tf_op jit(solution)/shard_map/psum | solution.py:38
  249.4 155.5 %all-gather.6.cloned.1.call-start = ((), (), s32[]{:S(2)}) async-start(), calls=%async_computation.4 | async-start | bytes 17039360 | tf_op jit(solution)/shard_map/all_gather | solution.py:40
  404.9 67.1 %copy-start.1 = (f32[128,256]{0,1:T(8,128)S(1)}, f32[128,256]{0,1:T(8,128)}, u32[]{:S(2)}) copy-start(f32[128,256]{0,1:T(8,128)} %all-reduce.4.cloned.1.call-done) | copy-start | bytes 393220
Sparse Core Ops, SparseCore 0:
  10.8 83.1 all-gather.3
  105.8 143.5 reduce-scatter.1
  251.8 47.1 all-reduce.3
  302.2 102.6 all-gather.5
